TPU v7x, 512 devices: a whole 4x4x16 slice. The times are simulated.
512 devices in a mesh: row: 16 (over y_hi, x, core), col: 32 (over y_lo, z).
Axes of the slice: x: 4, y: 4 (y_hi: 2, y_lo: 2; y = y_hi * 2 + y_lo), z: 16, core: 2. Of those that a mesh axis runs over, the one named last changes fastest.
Arguments:
- eri: bfloat16 [128, 40, 40, 4096], P('row', None, None, 'col'), may hold values from -6 to 6
- slot_tile: int32 [128], P('row'), may hold values from 0 to 225, as said below
- tile_mask: int32 [225], replicated, may hold values from 0 to 1, as said below
- coef_mu: bfloat16 [600, 8], replicated, may hold values from -0.25 to 0.25
- coef_lam: bfloat16 [1024, 8], P('col'), may hold values from -0.1875 to 0.1875
Outputs:
- half_mo: float32 [32, 4800], P('col', 'row')
Inputs may be any that keep to these rules, and one draw needn't show every extreme that they name: `slot_tile`: each tile (a, b) with a <= b of the 15 x 15 grid, written a * 15 + b, stands in exactly one slot; every other slot holds 225. `tile_mask`: entries of tiles below the diagonal (a > b) are 0.
All inputs are finite; a program needn't handle non-finite values.
Results may differ from a plain program's by a relative error of at most 0.0003.
Values sent between devices are 32-bit elements; how exact they have to be, the bound alone decides.
A program may use at most 64 MiB of HBM per device.

v0:
```python
import jax
import jax.numpy as jnp
from jax import lax
from jax.sharding import PartitionSpec as P

SW = 4


def per_device(eri, slot_tile, tile_mask, coef_mu, coef_lam):
    slot_count, tile_edge, unused_edge, pair_width = eri.shape
    basis_count, occupied = coef_mu.shape
    nblocks = basis_count // tile_edge
    tile_count = nblocks * nblocks
    mu_block = slot_tile // nblocks
    nu_block = slot_tile % nblocks
    matches = slot_tile[:, None] == jnp.arange(tile_count, dtype=jnp.int32)[None, :]
    screen = jnp.sum(jnp.where(matches, tile_mask[None, :], 0), axis=1).astype(jnp.float32)
    block_ids = jnp.arange(nblocks, dtype=jnp.int32)[None, :]
    pick_first = (mu_block[:, None] == block_ids).astype(jnp.float32)
    pick_second = (nu_block[:, None] == block_ids).astype(jnp.float32)
    table = coef_mu.reshape(nblocks, tile_edge * occupied)
    coef_first = jnp.dot(pick_first.astype(jnp.bfloat16), table, preferred_element_type=jnp.float32)
    coef_first = coef_first.astype(jnp.bfloat16).reshape(slot_count, tile_edge, occupied)
    coef_second = jnp.dot(
        pick_second.astype(jnp.bfloat16), table, preferred_element_type=jnp.float32
    )
    coef_second = coef_second.astype(jnp.bfloat16).reshape(slot_count, tile_edge, occupied)
    direct = jnp.einsum("spi,spqx->siqx", coef_first, eri, preferred_element_type=jnp.float32)
    mirrored = jnp.einsum("sqi,spqx->sipx", coef_second, eri, preferred_element_type=jnp.float32)
    place_direct = pick_second * screen[:, None]
    upper_only = (mu_block < nu_block).astype(jnp.float32)
    place_mirror = pick_first * (screen * upper_only)[:, None]
    partial_value = jnp.einsum(
        "sb,siqx->xibq", place_direct, direct, precision=lax.Precision.HIGHEST
    )
    partial_value = partial_value + jnp.einsum(
        "sb,sipx->xibp", place_mirror, mirrored, precision=lax.Precision.HIGHEST
    )
    partial_value = partial_value.reshape(pair_width, occupied * basis_count)
    coef_float = coef_lam.astype(jnp.float32)
    column_part = lax.psum_scatter(partial_value, "row", scatter_dimension=1, tiled=True)
    lambda_count = coef_lam.shape[0]
    products = jnp.einsum(
        "lj,lsc->jsc",
        coef_float,
        column_part.reshape(lambda_count, SW, -1),
        precision=lax.Precision.HIGHEST,
    )
    products = products.reshape(occupied * SW, -1)
    return lax.psum_scatter(products, "col", scatter_dimension=0, tiled=True)


def solution(mesh):
    in_specs = (P("row", None, None, "col"), P("row"), P(), P(), P("col", None))
    out_specs = P("col", "row")
    return jax.shard_map(
        per_device, mesh=mesh, in_specs=in_specs, out_specs=out_specs, check_vma=False
    )
```

profile of v0, /device:TPU:16, one launch (start us, length us, event | category | flops | bytes accessed | tf_op | source)
XLA Modules:
  0.0 202.3 jit_solution(3678099829623237949)
XLA Ops:
  0.0 0.0 copy-start
  0.0 1.0 select_reduce_fusion
  1.0 0.7 compare_select_fusion
  1.7 0.9 copy.21
  2.6 0.2 reshape.26
  2.7 0.2 convolution_convert_fusion.1
  2.9 0.1 reshape.27
  3.0 0.2 convolution_convert_fusion
  3.2 0.1 reshape.28
  3.4 0.0 copy-done
  3.4 0.6 fusion.1
  4.0 0.6 fusion.7
  4.7 2.9 %fusion.4 = f32[8,40,128,15]{2,3,1,0:T(8,128)S(1)} fusion(f32[8,8,40,128]{3,1,2,0:T(8,128)S(1)} %fusion.1, f32[8]{0:T(128)S(1)} %convert_element_type.30, s32[8]{0:T(128)S(1)} %get-tuple-element.6), kind=kOutput, calls=%fused_computation.4 | convolution fusion | flops 58982640 | bytes 3768384 | tf_op jit(solution)/shard_map/sb,siqx->xibq/dot_general | solution.py:33
  7.6 2.9 %add_bitcast_fusion = f32[128,8,15,40]{0,2,3,1:T(8,128)S(1)} fusion(f32[8,40,128,15]{2,3,1,0:T(8,128)S(1)} %fusion.4, f32[8,8,40,128]{3,1,2,0:T(8,128)S(1)} %fusion.7, f32[8]{0:T(128)S(1)} %get-tuple-element.5, s32[8]{0:T(128)S(1)} %get-tuple-element.7), kind=kOutput, calls=%fused_computation.2 | convolution fusion | flops 59597040 | bytes 6225984 | tf_op jit(solution)/shard_map/sb,sipx->xibp/dot_general | solution.py:36
  10.5 2.2 %copy.27 = f32[128,8,15,40]{0,3,2,1:T(8,128)} copy(f32[128,8,15,40]{0,2,3,1:T(8,128)S(1)} %add_bitcast_fusion) | data formatting | bytes 4915200 | tf_op jit(solution)/shard_map/add | solution.py:36
  12.7 0.0 copy-start.1
  12.7 43.5 %fusion = f32[128,304]{0,1:T(8,128)S(1)} fusion(f32[128,4800]{0,1:T(8,128)} %bitcast.35), kind=kCustom, calls=%all-reduce-scatter | all-reduce-scatter fusion | flops 622593 | bytes 2615296
  56.2 1.9 collective-permute-start
  58.2 1.3 dynamic-slice.6
  60.1 1.3 dynamic-slice.2
  61.4 3.7 %collective-permute-done = f32[128,60]{0,1:T(8,128)S(1)} collective-permute-done((f32[128,60]{0,1:T(8,128)S(1)}, f32[128,60]{0,1:T(8,128)S(1)}, u32[]{:S(2)}, u32[]{:S(2)}) %collective-permute-start) | collective-permute-done | bytes 30752
  65.1 2.0 %concatenate = f32[128,364]{0,1:T(8,128)} concatenate(f32[128,60]{0,1:T(8,128)S(1)} %collective-permute-done, f32[128,304]{0,1:T(8,128)S(1)} %fusion), dimensions={1} | concatenate | bytes 372736
  67.1 1.6 constant_dynamic-slice_fusion
  68.7 1.0 copy.28
  69.8 0.7 reshape.30
  70.5 0.0 copy-done.1
  70.5 1.1 convolution_bitcast_fusion
  71.7 129.4 %all-reduce.1 = f32[32,300]{1,0:T(8,128)S(1)} all-reduce(f32[32,300]{1,0:T(8,128)S(1)} %reshape.31), channel_id=3, replica_groups=mesh['row'=16,'col'=32] {'col'}, use_global_device_ids=true, to_apply=%region_2.3.clone | all-reduce | flops 9600 | bytes 76800
  201.1 1.2 constant_dynamic-slice_fusion.1
  (4 shorter events, 0.0 us)
Async XLA Ops:
  0.0 3.4 %copy-start = (bf16[8,40,40,128]{3,2,1,0:T(8,128)(2,1)S(1)}, bf16[8,40,40,128]{3,2,1,0:T(8,128)(2,1)}, u32[]{:S(2)}) copy-start(bf16[8,40,40,128]{3,2,1,0:T(8,128)(2,1)} %param.5) | copy-start | bytes 9830404
  12.7 57.8 %copy-start.1 = (bf16[32,8]{0,1:T(8,128)(2,1)S(1)}, bf16[32,8]{0,1:T(8,128)(2,1)}, u32[]{:S(2)}) copy-start(bf16[32,8]{0,1:T(8,128)(2,1)} %param.9) | copy-start | bytes 1540
  56.2 8.8 %collective-permute-start = (f32[128,60]{0,1:T(8,128)S(1)}, f32[128,60]{0,1:T(8,128)S(1)}, u32[]{:S(2)}, u32[]{:S(2)}) collective-permute-start(f32[128,60]{0,1:T(8,128)S(1)} %slice), channel_id=1, source_target_pairs={{0,32},{32,64},{64,96},{96,128},{128,160},{160,192},{192,224},{224... | collective-permute-start | bytes 92168
where the time goes:
time: 203 us; the launch traced here: 202 us
  blocking collectives  173 us (85%)
  local copies, waits for them, and re-layouts  12.6 us (6%)
  matrix products  8.61 us (4%)
  waiting for transfers between devices  3.71 us (2%)
    unnamed x2, blocking collectives  173 us
    unnamed x11, local copies, waits for them, and re-layouts  8.26 us
  transfers between devices with their start and end apart: 1, of which 1 were waited for; matrix products, arithmetic and copies ran while one was open for 1% of the time, Pallas kernels for 0%

commit v1 on v0

v1 whole, which is shorter than its diff:
```python
import functools

import jax
import jax.numpy as jnp
from jax import lax
from jax.experimental import pallas as pl
from jax.experimental.pallas import tpu as pltpu
from jax.sharding import PartitionSpec as P

MESH = pl.DeviceIdType.MESH
SW = 4
F32 = jnp.float32
BF16 = jnp.bfloat16


def spread_coefficients(tile_ref, mask_ref, coef_ref, blocks, left, slots, edge, occ, nb):
    width = slots * edge
    for b in range(nb):
        blocks[b, :, :edge] = coef_ref[:, b * edge : (b + 1) * edge].astype(F32)
    lane = lax.broadcasted_iota(jnp.int32, (1, width), 1) // edge
    direct_parts, mirror_parts = [], []
    direct_target = jnp.full((1, width), -1, jnp.int32)
    mirror_target = jnp.full((1, width), -1, jnp.int32)
    for s in range(slots):
        tile = tile_ref[s]
        first, second = tile // nb, tile % nb
        valid = tile < nb * nb
        keep = jnp.where(valid & (mask_ref[jnp.minimum(tile, nb * nb - 1)] > 0), 1, 0)
        weight = keep.astype(F32)
        mirror = jnp.where(first < second, weight, 0.0)
        direct_parts.append(blocks[jnp.minimum(first, nb - 1)][:, :edge] * weight)
        mirror_parts.append(blocks[second][:, :edge] * mirror)
        direct_target = jnp.where(lane == s, second, direct_target)
        mirror_target = jnp.where(lane == s, first, mirror_target)
    gathered = jnp.concatenate(direct_parts + mirror_parts, axis=1)
    target = jnp.concatenate([direct_target, mirror_target], axis=1)
    row = lax.broadcasted_iota(jnp.int32, (8, 2 * width), 0)
    for half in range(2):
        for core in range(2):
            block = row + core * (8 - half)
            hit = target == block
            rows = []
            for i in range(occ):
                rows.append(jnp.where(hit, gathered[i : i + 1, :], 0.0).astype(BF16))
            left[half, pl.ds(core * 8 * occ, 8 * occ), :] = jnp.concatenate(rows, axis=0)


def kernel(
    eri_ref, tile_ref, mask_ref, coef_ref, lam_ref, out_ref,
    ebuf, eturn, blocks, left, acc, theirs, mine, got_core, send_plane, got_plane, send_z, got_z,
    load_sem, core_send, core_recv, plane_send, plane_recv, z_send, z_recv,
):
    slots, edge, unused, pairs = eri_ref.shape
    occ, basis = coef_ref.shape
    nb = basis // edge
    half_edge = edge // 2
    lams = lam_ref.shape[1]
    row, col = lax.axis_index("row"), lax.axis_index("col")
    core, orbital = row % 2, row // 2
    jhi, z = col // 16, col % 16
    place = orbital * 2 + jhi

    load = pltpu.make_async_copy(eri_ref, ebuf, load_sem)
    load.start()

    barrier = pltpu.get_barrier_semaphore()
    pl.semaphore_signal(barrier, inc=1, device_id=(orbital * 2 + 1 - core, col), device_id_type=MESH)

    def greet(d, unused):
        other = place ^ d
        pl.semaphore_signal(
            barrier, inc=1, device_id=((other // 2) * 2 + core, (other % 2) * 16 + z), device_id_type=MESH
        )
        pl.semaphore_signal(barrier, inc=1, device_id=(row, jhi * 16 + (z ^ d)), device_id_type=MESH)
        return unused

    lax.fori_loop(1, 16, greet, 0)

    spread_coefficients(tile_ref, mask_ref, coef_ref, blocks, left, slots, edge, occ, nb)

    rows_l = lax.broadcasted_iota(jnp.int32, (lams, pairs), 0)
    cols_l = lax.broadcasted_iota(jnp.int32, (lams, pairs), 1)
    widen = jnp.where(rows_l == cols_l // SW, 1.0, 0.0).astype(BF16)
    by_pair = jnp.dot(lam_ref[...], widen, preferred_element_type=F32)
    rows_j = lax.broadcasted_iota(jnp.int32, (occ * SW, occ), 0)
    cols_j = lax.broadcasted_iota(jnp.int32, (occ * SW, occ), 1)
    repeat = jnp.where(rows_j // SW == cols_j, 1.0, 0.0).astype(BF16)
    by_row = jnp.dot(repeat, by_pair.astype(BF16), preferred_element_type=F32)
    rows_s = lax.broadcasted_iota(jnp.int32, (occ * SW, pairs), 0)
    cols_s = lax.broadcasted_iota(jnp.int32, (occ * SW, pairs), 1)
    lam_mat = jnp.where(rows_s % SW == cols_s % SW, by_row, 0.0).astype(BF16)
    lam_twice = jnp.concatenate([lam_mat, lam_mat], axis=1)

    load.wait()
    for s in range(slots):
        eturn[:, s * edge : (s + 1) * edge, :] = jnp.swapaxes(ebuf[s], 0, 1)

    def transform(step, unused):
        for half in range(2):
            at = [step * 2, step * 2 + 1]
            right = jnp.concatenate(
                [
                    jnp.concatenate(
                        [eturn[half * half_edge + u], ebuf[:, half * half_edge + u].reshape(slots * edge, pairs)], axis=0
                    )
                    for u in at
                ],
                axis=1,
            )
            sums = jnp.dot(left[half], right, preferred_element_type=F32)
            for n, u in enumerate(at):
                for c in range(2):
                    start = (half ^ c) * half_edge + u
                    for i in range(occ):
                        g = c * occ + i
                        acc[g, pl.ds(start, 8, stride=edge), :] = sums[g * 8 : g * 8 + 8, n * pairs : (n + 1) * pairs]
        return unused

    lax.fori_loop(0, half_edge // 2, transform, 0)

    def contract(c, i):
        value = acc[c * occ + i]
        high = value.astype(BF16)
        low = (value - high.astype(F32)).astype(BF16)
        both = jnp.concatenate([high, low], axis=1)
        got = lax.dot_general(lam_twice, both, (((1,), (1,)), ((), ())), preferred_element_type=F32)
        return jnp.concatenate([got, jnp.zeros((occ * SW, 64), F32)], axis=1)

    pl.semaphore_wait(barrier, 31)
    core_copies = []
    for i in range(occ):
        got = contract(1 - core, i)
        theirs[2 * i] = got[:16]
        theirs[2 * i + 1] = got[16:]
        copy = pltpu.make_async_remote_copy(
            src_ref=theirs.at[pl.ds(2 * i, 2)],
            dst_ref=got_core.at[pl.ds(2 * i, 2)],
            send_sem=core_send.at[i],
            recv_sem=core_recv.at[i],
            device_id=(orbital * 2 + 1 - core, col),
            device_id_type=MESH,
        )
        copy.start()
        core_copies.append(copy)
    for i in range(occ):
        got = contract(core, i)
        mine[2 * i] = got[:16]
        mine[2 * i + 1] = got[16:]
    for copy in core_copies:
        copy.wait()

    plane_copies = []
    for d in range(1, 16):
        other = place ^ d
        send_plane[d] = mine[other] + got_core[other]
        copy = pltpu.make_async_remote_copy(
            src_ref=send_plane.at[d],
            dst_ref=got_plane.at[d],
            send_sem=plane_send.at[d],
            recv_sem=plane_recv.at[d],
            device_id=((other // 2) * 2 + core, (other % 2) * 16 + z),
            device_id_type=MESH,
        )
        copy.start()
        plane_copies.append(copy)
    total = mine[place] + got_core[place]
    for d in range(1, 16):
        plane_copies[d - 1].wait()
        total = total + got_plane[d]

    for k in range(3):
        send_z[:, k, :] = total[:, k * 128 : (k + 1) * 128]
    z_copies = []
    for d in range(1, 16):
        copy = pltpu.make_async_remote_copy(
            src_ref=send_z.at[z ^ d],
            dst_ref=got_z.at[d],
            send_sem=z_send.at[d],
            recv_sem=z_recv.at[d],
            device_id=(row, jhi * 16 + (z ^ d)),
            device_id_type=MESH,
        )
        copy.start()
        z_copies.append(copy)
    final = send_z[z]
    for d in range(1, 16):
        z_copies[d - 1].wait()
        final = final + got_z[d]
    out_ref[...] = final


def per_device(eri, slot_tile, tile_mask, coef_mu, coef_lam):
    slots, edge, unused, pairs = eri.shape
    basis, occ = coef_mu.shape
    nb = basis // edge
    smem = pl.BlockSpec(memory_space=pltpu.SMEM)
    vmem = pl.BlockSpec(memory_space=pltpu.VMEM)
    result = pl.pallas_call(
        kernel,
        out_shape=jax.ShapeDtypeStruct((3, 128), F32),
        in_specs=[pl.BlockSpec(memory_space=pl.ANY), smem, smem, vmem, vmem],
        out_specs=vmem,
        scratch_shapes=[
            pltpu.VMEM((slots, edge, edge, pairs), BF16),
            pltpu.VMEM((edge, slots * edge, pairs), BF16),
            pltpu.VMEM((nb, occ, 128), F32),
            pltpu.VMEM((2, 16 * occ, 2 * slots * edge), BF16),
            pltpu.VMEM((2 * occ, 8 * edge, pairs), F32),
            pltpu.VMEM((16, 16, 384), F32),
            pltpu.VMEM((16, 16, 384), F32),
            pltpu.VMEM((16, 16, 384), F32),
            pltpu.VMEM((16, 16, 384), F32),
            pltpu.VMEM((16, 16, 384), F32),
            pltpu.VMEM((16, 3, 128), F32),
            pltpu.VMEM((16, 3, 128), F32),
            pltpu.SemaphoreType.DMA,
            pltpu.SemaphoreType.DMA((occ,)),
            pltpu.SemaphoreType.DMA((occ,)),
            pltpu.SemaphoreType.DMA((16,)),
            pltpu.SemaphoreType.DMA((16,)),
            pltpu.SemaphoreType.DMA((16,)),
            pltpu.SemaphoreType.DMA((16,)),
        ],
        compiler_params=pltpu.CompilerParams(
            collective_id=0, has_side_effects=True, vmem_limit_bytes=56 * 2**20
        ),
    )(eri, slot_tile, tile_mask, coef_mu.T, coef_lam.T)
    return result.reshape(1, 384)[:, :300]


def solution(mesh):
    in_specs = (P("row", None, None, "col"), P("row"), P(), P(), P("col", None))
    out_specs = P("col", "row")
    return jax.shard_map(
        per_device, mesh=mesh, in_specs=in_specs, out_specs=out_specs, check_vma=False
    )
```

time: 203 us -> 38.7 us (0.19)
  the two profiles are of different devices: /device:TPU:16 before, /device:TPU:1 now
where the time goes in v1:
time: 38.7 us; the launch traced here: 38.4 us
  Pallas kernels  37.2 us (96%)
  local copies, waits for them, and re-layouts  1.25 us (3%)
    pallas_call x1, Pallas kernels, per_device(): pl.pallas_call(kernel, out_shape=jax.ShapeDtypeStruct((3, 128), F32), in_...  37.2 us
    unnamed x1, local copies, waits for them, and re-layouts  1.25 us

profile of v1, /device:TPU:1, one launch (start us, length us, event | category | flops | bytes accessed | tf_op | source)
XLA Modules:
  0.0 38.4 jit_solution(17337034191866114441)
XLA Ops:
  0.0 37.2 %shard_map.55 = f32[3,128]{1,0:T(4,128)} custom-call(bf16[8,40,40,128]{3,2,1,0:T(8,128)(2,1)} %eri_ref.1, s32[8]{0:T(128)} %tile_ref.1, s32[225]{0:T(256)} %mask_ref.1, bf16[8,600]{1,0:T(8,128)(2,1)} %bitcast.8, bf16[8,32]{1,0:T(8,128)(2,1)} %bitcast.10), custom_call_target="tpu_custom_call" | custom-call | tf_op jit(solution)/shard_map/pallas_call | solution.py:198
  37.2 1.2 %copy.8 = f32[1,1,3,128]{3,1,2,0:T(1,128)} copy(f32[1,1,3,128]{3,2,1,0:T(4,128)} %bitcast.9) | data formatting | bytes 3072

commit v2 on v1

--- a/solution.py
+++ b/solution.py
@@ -9,6 +9,11 @@
 
 MESH = pl.DeviceIdType.MESH
 SW = 4
+PLANE_HOPS = (0, 1, 2, 1)
+PLANE_ORDER = sorted(
+    range(1, 16), key=lambda d: -(PLANE_HOPS[d // 8 * 2 + d % 2] + PLANE_HOPS[d // 2 % 4])
+)
+Z_ORDER = [8, 7, 9, 6, 10, 5, 11, 4, 12, 3, 13, 2, 14, 1, 15]
 F32 = jnp.float32
 BF16 = jnp.bfloat16
 
@@ -46,11 +51,11 @@
 
 
 def kernel(
-    eri_ref, tile_ref, mask_ref, coef_ref, lam_ref, out_ref,
-    ebuf, eturn, blocks, left, acc, theirs, mine, got_core, send_plane, got_plane, send_z, got_z,
-    load_sem, core_send, core_recv, plane_send, plane_recv, z_send, z_recv,
+    eri_hbm, tile_hbm, mask_hbm, coef_hbm, lam_hbm, out_ref,
+    tile_ref, mask_ref, coef_ref, lam_ref, ebuf, eturn, blocks, left, acc, theirs, mine, got_core, send_plane, got_plane, send_z, got_z,
+    load_sem, small_sem, core_send, core_recv, plane_send, plane_recv, z_send, z_recv,
 ):
-    slots, edge, unused, pairs = eri_ref.shape
+    slots, edge, unused, pairs = ebuf.shape
     occ, basis = coef_ref.shape
     nb = basis // edge
     half_edge = edge // 2
@@ -60,8 +65,17 @@
     jhi, z = col // 16, col % 16
     place = orbital * 2 + jhi
 
-    load = pltpu.make_async_copy(eri_ref, ebuf, load_sem)
-    load.start()
+    smalls = [
+        pltpu.make_async_copy(a, b, small_sem.at[n])
+        for n, (a, b) in enumerate(
+            [(tile_hbm, tile_ref), (mask_hbm, mask_ref), (coef_hbm, coef_ref), (lam_hbm, lam_ref)]
+        )
+    ]
+    for copy in smalls:
+        copy.start()
+    loads = [pltpu.make_async_copy(eri_hbm.at[s], ebuf.at[s], load_sem.at[s]) for s in range(slots)]
+    for copy in loads:
+        copy.start()
 
     barrier = pltpu.get_barrier_semaphore()
     pl.semaphore_signal(barrier, inc=1, device_id=(orbital * 2 + 1 - core, col), device_id_type=MESH)
@@ -76,6 +90,8 @@
 
     lax.fori_loop(1, 16, greet, 0)
 
+    for copy in smalls:
+        copy.wait()
     spread_coefficients(tile_ref, mask_ref, coef_ref, blocks, left, slots, edge, occ, nb)
 
     rows_l = lax.broadcasted_iota(jnp.int32, (lams, pairs), 0)
@@ -91,11 +107,11 @@
     lam_mat = jnp.where(rows_s % SW == cols_s % SW, by_row, 0.0).astype(BF16)
     lam_twice = jnp.concatenate([lam_mat, lam_mat], axis=1)
 
-    load.wait()
     for s in range(slots):
+        loads[s].wait()
         eturn[:, s * edge : (s + 1) * edge, :] = jnp.swapaxes(ebuf[s], 0, 1)
 
-    def transform(step, unused):
+    for step in range(half_edge // 2):
         for half in range(2):
             at = [step * 2, step * 2 + 1]
             right = jnp.concatenate(
@@ -114,9 +130,6 @@
                     for i in range(occ):
                         g = c * occ + i
                         acc[g, pl.ds(start, 8, stride=edge), :] = sums[g * 8 : g * 8 + 8, n * pairs : (n + 1) * pairs]
-        return unused
-
-    lax.fori_loop(0, half_edge // 2, transform, 0)
 
     def contract(c, i):
         value = acc[c * occ + i]
@@ -150,7 +163,7 @@
         copy.wait()
 
     plane_copies = []
-    for d in range(1, 16):
+    for d in PLANE_ORDER:
         other = place ^ d
         send_plane[d] = mine[other] + got_core[other]
         copy = pltpu.make_async_remote_copy(
@@ -164,43 +177,49 @@
         copy.start()
         plane_copies.append(copy)
     total = mine[place] + got_core[place]
-    for d in range(1, 16):
-        plane_copies[d - 1].wait()
+    for copy, d in zip(plane_copies, PLANE_ORDER):
+        copy.wait_recv()
         total = total + got_plane[d]
 
     for k in range(3):
         send_z[:, k, :] = total[:, k * 128 : (k + 1) * 128]
     z_copies = []
-    for d in range(1, 16):
+    for d in Z_ORDER:
         copy = pltpu.make_async_remote_copy(
-            src_ref=send_z.at[z ^ d],
+            src_ref=send_z.at[(z + d) % 16],
             dst_ref=got_z.at[d],
             send_sem=z_send.at[d],
             recv_sem=z_recv.at[d],
-            device_id=(row, jhi * 16 + (z ^ d)),
+            device_id=(row, jhi * 16 + (z + d) % 16),
             device_id_type=MESH,
         )
         copy.start()
         z_copies.append(copy)
     final = send_z[z]
-    for d in range(1, 16):
-        z_copies[d - 1].wait()
+    for copy, d in zip(z_copies, Z_ORDER):
+        copy.wait_recv()
         final = final + got_z[d]
-    out_ref[...] = final
+    for k in range(3):
+        width = min(128, 300 - 128 * k)
+        out_ref[:, k * 128 : k * 128 + width] = final[k : k + 1, :width]
+    for copy in plane_copies + z_copies:
+        copy.wait_send()
 
 
 def per_device(eri, slot_tile, tile_mask, coef_mu, coef_lam):
     slots, edge, unused, pairs = eri.shape
     basis, occ = coef_mu.shape
     nb = basis // edge
-    smem = pl.BlockSpec(memory_space=pltpu.SMEM)
-    vmem = pl.BlockSpec(memory_space=pltpu.VMEM)
-    result = pl.pallas_call(
+    return pl.pallas_call(
         kernel,
-        out_shape=jax.ShapeDtypeStruct((3, 128), F32),
-        in_specs=[pl.BlockSpec(memory_space=pl.ANY), smem, smem, vmem, vmem],
-        out_specs=vmem,
+        out_shape=pltpu.VMEM((1, 300), F32),
+        in_specs=[pl.BlockSpec(memory_space=pltpu.HBM)] * 5,
+        out_specs=pl.BlockSpec(memory_space=pltpu.VMEM),
         scratch_shapes=[
+            pltpu.SMEM(slot_tile.shape, jnp.int32),
+            pltpu.SMEM(tile_mask.shape, jnp.int32),
+            pltpu.VMEM((occ, basis), BF16),
+            pltpu.VMEM((occ, coef_lam.shape[0]), BF16),
             pltpu.VMEM((slots, edge, edge, pairs), BF16),
             pltpu.VMEM((edge, slots * edge, pairs), BF16),
             pltpu.VMEM((nb, occ, 128), F32),
@@ -213,7 +232,8 @@
             pltpu.VMEM((16, 16, 384), F32),
             pltpu.VMEM((16, 3, 128), F32),
             pltpu.VMEM((16, 3, 128), F32),
-            pltpu.SemaphoreType.DMA,
+            pltpu.SemaphoreType.DMA((slots,)),
+            pltpu.SemaphoreType.DMA((4,)),
             pltpu.SemaphoreType.DMA((occ,)),
             pltpu.SemaphoreType.DMA((occ,)),
             pltpu.SemaphoreType.DMA((16,)),
@@ -225,7 +245,6 @@
             collective_id=0, has_side_effects=True, vmem_limit_bytes=56 * 2**20
         ),
     )(eri, slot_tile, tile_mask, coef_mu.T, coef_lam.T)
-    return result.reshape(1, 384)[:, :300]
 
 
 def solution(mesh):

time: 38.7 us -> 33.8 us (0.87)
  Pallas kernels: 37.2 us -> 33.1 us
  local copies, waits for them, and re-layouts: 1.25 us -> 0.56 us
    pallas_call x1, Pallas kernels: 37.2 us -> 33.1 us  [per_device(): pl.pallas_call(kernel, out_shape=pltpu.VMEM((1, 300), F32), in_specs=[pl....]
    unnamed x1, local copies, waits for them, and re-layouts: 1.25 us -> 0.56 us
where the time goes in v2:
time: 33.8 us; the launch traced here: 33.7 us
  Pallas kernels  33.1 us (98%)
  local copies, waits for them, and re-layouts  0.56 us (2%)
    pallas_call x1, Pallas kernels, per_device(): pl.pallas_call(kernel, out_shape=pltpu.VMEM((1, 300), F32), in_specs=[pl....  33.1 us

profile of v2, /device:TPU:1, one launch (start us, length us, event | category | flops | bytes accessed | tf_op | source)
XLA Modules:
  0.0 33.7 jit_solution(13331242160610866214)
XLA Ops:
  0.0 33.1 %shard_map.55 = f32[1,300]{1,0:T(1,128)S(1)} custom-call(bf16[8,40,40,128]{3,2,1,0:T(8,128)(2,1)} %eri_hbm.1, s32[8]{0:T(128)} %tile_hbm.1, s32[225]{0:T(256)} %mask_hbm.1, bf16[8,600]{1,0:T(8,128)(2,1)} %bitcast.2, bf16[8,32]{1,0:T(8,128)(2,1)} %bitcast.3), custom_call_target="tpu_custom_call" | custom-call | tf_op jit(solution)/shard_map/pallas_call | solution.py:213
  33.1 0.6 %copy.7 = f32[1,300]{1,0:T(1,128)} copy(f32[1,300]{1,0:T(1,128)S(1)} %shard_map.55) | data formatting | bytes 2400

commit v3 on v2

v3 whole, which is shorter than its diff:
```python
import functools

import jax
import jax.numpy as jnp
from jax import lax
from jax.experimental import pallas as pl
from jax.experimental.pallas import tpu as pltpu
from jax.sharding import PartitionSpec as P

MESH = pl.DeviceIdType.MESH
SW = 4
PLANE_HOPS = (0, 1, 2, 1)
PLANE_ORDER = sorted(
    range(1, 16), key=lambda d: -(PLANE_HOPS[d // 8 * 2 + d % 2] + PLANE_HOPS[d // 2 % 4])
)
Z_ORDER = [8, 7, 9, 6, 10, 5, 11, 4, 12, 3, 13, 2, 14, 1, 15]
F32 = jnp.float32
BF16 = jnp.bfloat16


def spread_coefficients(tile_ref, mask_ref, coef_ref, blocks, left, slots, edge, occ, nb):
    width = slots * edge
    for b in range(nb):
        blocks[b, :, :edge] = coef_ref[:, b * edge : (b + 1) * edge].astype(F32)
    lane = lax.broadcasted_iota(jnp.int32, (1, width), 1) // edge
    direct_parts, mirror_parts = [], []
    direct_target = jnp.full((1, width), -1, jnp.int32)
    mirror_target = jnp.full((1, width), -1, jnp.int32)
    for s in range(slots):
        tile = tile_ref[s]
        first, second = tile // nb, tile % nb
        valid = tile < nb * nb
        keep = jnp.where(valid & (mask_ref[jnp.minimum(tile, nb * nb - 1)] > 0), 1, 0)
        weight = keep.astype(F32)
        mirror = jnp.where(first < second, weight, 0.0)
        direct_parts.append(blocks[jnp.minimum(first, nb - 1)][:, :edge] * weight)
        mirror_parts.append(blocks[second][:, :edge] * mirror)
        direct_target = jnp.where(lane == s, second, direct_target)
        mirror_target = jnp.where(lane == s, first, mirror_target)
    gathered = jnp.concatenate(direct_parts + mirror_parts, axis=1)
    target = jnp.concatenate([direct_target, mirror_target], axis=1)
    row = lax.broadcasted_iota(jnp.int32, (8, 2 * width), 0)
    for half in range(2):
        for core in range(2):
            block = row + core * (8 - half)
            hit = target == block
            rows = []
            for i in range(occ):
                rows.append(jnp.where(hit, gathered[i : i + 1, :], 0.0).astype(BF16))
            left[half, pl.ds(core * 8 * occ, 8 * occ), :] = jnp.concatenate(rows, axis=0)


def second_factor(lam_ref, pairs, occ):
    lams = lam_ref.shape[1]
    rows_l = lax.broadcasted_iota(jnp.int32, (lams, pairs), 0)
    cols_l = lax.broadcasted_iota(jnp.int32, (lams, pairs), 1)
    widen = jnp.where(rows_l == cols_l // SW, 1.0, 0.0).astype(BF16)
    by_pair = jnp.dot(lam_ref[...], widen, preferred_element_type=F32)
    rows_j = lax.broadcasted_iota(jnp.int32, (occ * SW, occ), 0)
    cols_j = lax.broadcasted_iota(jnp.int32, (occ * SW, occ), 1)
    repeat = jnp.where(rows_j // SW == cols_j, 1.0, 0.0).astype(BF16)
    by_row = jnp.dot(repeat, by_pair.astype(BF16), preferred_element_type=F32)
    rows_s = lax.broadcasted_iota(jnp.int32, (occ * SW, pairs), 0)
    cols_s = lax.broadcasted_iota(jnp.int32, (occ * SW, pairs), 1)
    lam_mat = jnp.where(rows_s % SW == cols_s % SW, by_row, 0.0).astype(BF16)
    return jnp.concatenate([lam_mat, lam_mat], axis=1)


def output_order(order, z, edge):
    shape = order.shape
    k = lax.broadcasted_iota(jnp.int32, shape, 0)
    n = lax.broadcasted_iota(jnp.int32, shape, 1)
    tile, lane = k // 128, k % 128
    block = lane % 8
    wide = (lane // 64) * (edge // 2) + (lane // 8) % 8 + 8 * tile
    narrow = (lane // 32) % 2 * (edge // 2) + (lane // 8) % 4 + 16
    narrow = jnp.where(lane // 64 == z // 8, narrow, -1024)
    column = block * edge + jnp.where(tile < 2, wide, narrow)
    order[...] = jnp.where(column == n, 1.0, 0.0).astype(BF16)


def kernel(
    eri_hbm, tile_hbm, mask_hbm, coef_hbm, lam_hbm, out_ref,
    tile_ref, mask_ref, coef_ref, lam_ref, ebuf, eturn, blocks, left, order, acc_a, acc_b, acc_c,
    theirs_p, theirs_q, mine_p, mine_q, core_p, core_q, send_p, send_q, got_p, got_q, send_z, got_z,
    load_sem, small_sem, core_send, core_recv, p_send, p_recv, q_send, q_recv, z_send, z_recv,
):
    slots, edge, unused, pairs = ebuf.shape
    occ, basis = coef_ref.shape
    nb = basis // edge
    half_edge = edge // 2
    row, col = lax.axis_index("row"), lax.axis_index("col")
    core, orbital = row % 2, row // 2
    jhi, z = col // 16, col % 16
    place = orbital * 2 + jhi
    sibling = (orbital * 2 + 1 - core, col)

    smalls = [
        pltpu.make_async_copy(a, b, small_sem.at[n])
        for n, (a, b) in enumerate(
            [(tile_hbm, tile_ref), (mask_hbm, mask_ref), (coef_hbm, coef_ref), (lam_hbm, lam_ref)]
        )
    ]
    for copy in smalls:
        copy.start()
    loads = [pltpu.make_async_copy(eri_hbm.at[s], ebuf.at[s], load_sem.at[s]) for s in range(slots)]
    for copy in loads:
        copy.start()

    barrier = pltpu.get_barrier_semaphore()
    pl.semaphore_signal(barrier, inc=1, device_id=sibling, device_id_type=MESH)

    def greet(d, unused):
        other = place ^ d
        pl.semaphore_signal(
            barrier, inc=1, device_id=((other // 2) * 2 + core, (other % 2) * 16 + z), device_id_type=MESH
        )
        pl.semaphore_signal(barrier, inc=1, device_id=(row, jhi * 16 + (z ^ d)), device_id_type=MESH)
        return unused

    lax.fori_loop(1, 16, greet, 0)

    output_order(order, z, edge)
    for copy in smalls:
        copy.wait()
    spread_coefficients(tile_ref, mask_ref, coef_ref, blocks, left, slots, edge, occ, nb)
    lam_twice = second_factor(lam_ref, pairs, occ)

    for s in range(slots):
        loads[s].wait()
        eturn[:, s * edge : (s + 1) * edge, :] = jnp.swapaxes(ebuf[s], 0, 1)

    def transform(acc, first, count):
        for half in range(2):
            for step in range(0, count, 2):
                base = half * half_edge + first + step
                right = jnp.concatenate(
                    [
                        jnp.concatenate([eturn[u], ebuf[:, u].reshape(slots * edge, pairs)], axis=0)
                        for u in (base, base + 1)
                    ],
                    axis=1,
                )
                sums = jnp.dot(left[half], right, preferred_element_type=F32)
                for c in range(2):
                    start = ((half ^ c) * count + step) * 8
                    for i in range(occ):
                        g = (c * occ + i) * 8
                        both = jnp.concatenate([sums[g : g + 8, :pairs], sums[g : g + 8, pairs:]], axis=0)
                        high = both.astype(BF16)
                        low = (both - high.astype(F32)).astype(BF16)
                        at = i * 2 * count * 8 + start
                        acc[c, at : at + 16, :pairs] = high
                        acc[c, at : at + 16, pairs:] = low

    def contract(acc, c, n):
        right = acc[c, n * 256 : n * 256 + 256, :]
        return lax.dot_general(lam_twice, right, (((1,), (1,)), ((), ())), preferred_element_type=F32)

    def contract_wide(acc, c, dest):
        for n in range(occ // 2):
            got = contract(acc, c, n)
            for k in range(2):
                for h in range(2):
                    dest[4 * n + 2 * k + h, 0:16, :] = got[16 * h : 16 * h + 16, 128 * k : 128 * k + 128]

    def contract_narrow(acc, c, dest):
        low_lanes = lax.broadcasted_iota(jnp.int32, (8, 128), 1) < 64
        for n in range(occ // 4):
            got = contract(acc, c, n)
            for k in range(2):
                for h in range(2):
                    below = got[16 * h : 16 * h + 8, 128 * k : 128 * k + 128]
                    above = got[16 * h + 8 : 16 * h + 16, 128 * k : 128 * k + 128]
                    m = 8 * n + 4 * k + h
                    dest[m, 16:24, :] = jnp.where(low_lanes, below, pltpu.roll(above, 64, 1))
                    dest[m + 2, 16:24, :] = jnp.where(low_lanes, pltpu.roll(below, 64, 1), above)

    def swap_cores(source, dest, n):
        copy = pltpu.make_async_remote_copy(
            src_ref=source, dst_ref=dest, send_sem=core_send.at[n], recv_sem=core_recv.at[n],
            device_id=sibling, device_id_type=MESH,
        )
        copy.start()
        return copy

    def share(mine, theirs, send, got, send_sem, recv_sem):
        copies = []
        for d in PLANE_ORDER:
            other = place ^ d
            send[d] = mine[other] + theirs[other]
            copy = pltpu.make_async_remote_copy(
                src_ref=send.at[d],
                dst_ref=got.at[d],
                send_sem=send_sem.at[d],
                recv_sem=recv_sem.at[d],
                device_id=((other // 2) * 2 + core, (other % 2) * 16 + z),
                device_id_type=MESH,
            )
            copy.start()
            copies.append(copy)
        return copies

    def gather(mine, theirs, got, copies):
        total = mine[place] + theirs[place]
        for copy, d in zip(copies, PLANE_ORDER):
            copy.wait_recv()
            total = total + got[d]
        return total

    transform(acc_a, 0, 8)
    contract_wide(acc_a, 1 - core, theirs_p)
    pl.semaphore_wait(barrier, 31)
    first_swap = swap_cores(theirs_p, core_p, 0)
    contract_wide(acc_a, core, mine_p)
    transform(acc_b, 8, 8)
    transform(acc_c, 16, 4)
    contract_wide(acc_b, 1 - core, theirs_q)
    contract_narrow(acc_c, 1 - core, theirs_q)
    second_swap = swap_cores(theirs_q, core_q, 1)
    first_swap.wait_recv()
    p_copies = share(mine_p, core_p, send_p, got_p, p_send, p_recv)
    contract_wide(acc_b, core, mine_q)
    contract_narrow(acc_c, core, mine_q)
    second_swap.wait_recv()
    q_copies = share(mine_q, core_q, send_q, got_q, q_send, q_recv)

    total = gather(mine_p, core_p, got_p, p_copies)
    send_z[:, 0, :] = total
    total = gather(mine_q, core_q, got_q, q_copies)
    send_z[:, 1, :] = total[:16]
    send_z[0:8, 2, :] = total[16:]
    send_z[8:16, 2, :] = total[16:]
    z_copies = []
    for d in Z_ORDER:
        other = (z + d) % 16
        copy = pltpu.make_async_remote_copy(
            src_ref=send_z.at[other],
            dst_ref=got_z.at[d],
            send_sem=z_send.at[d],
            recv_sem=z_recv.at[d],
            device_id=(row, jhi * 16 + other),
            device_id_type=MESH,
        )
        copy.start()
        z_copies.append(copy)
    final = send_z[z]
    for copy, d in zip(z_copies, Z_ORDER):
        copy.wait_recv()
        final = final + got_z[d]
    flat = jnp.concatenate([final[k : k + 1, :] for k in range(3)], axis=1)
    high = flat.astype(BF16)
    rest = flat - high.astype(F32)
    middle = rest.astype(BF16)
    low = (rest - middle.astype(F32)).astype(BF16)
    terms = jnp.concatenate([high, middle, low], axis=0)
    picked = jnp.dot(terms, order[...], preferred_element_type=F32)
    out_ref[...] = (picked[0:1] + picked[1:2] + picked[2:3])[:, : out_ref.shape[1]]
    for copy in [first_swap, second_swap] + p_copies + q_copies + z_copies:
        copy.wait_send()


def per_device(eri, slot_tile, tile_mask, coef_mu, coef_lam):
    slots, edge, unused, pairs = eri.shape
    basis, occ = coef_mu.shape
    nb = basis // edge
    return pl.pallas_call(
        kernel,
        out_shape=pltpu.VMEM((1, 300), F32),
        in_specs=[pl.BlockSpec(memory_space=pltpu.HBM)] * 5,
        out_specs=pl.BlockSpec(memory_space=pltpu.VMEM),
        scratch_shapes=[
            pltpu.SMEM(slot_tile.shape, jnp.int32),
            pltpu.SMEM(tile_mask.shape, jnp.int32),
            pltpu.VMEM((occ, basis), BF16),
            pltpu.VMEM((occ, coef_lam.shape[0]), BF16),
            pltpu.VMEM((slots, edge, edge, pairs), BF16),
            pltpu.VMEM((edge, slots * edge, pairs), BF16),
            pltpu.VMEM((nb, occ, 128), F32),
            pltpu.VMEM((2, 16 * occ, 2 * slots * edge), BF16),
            pltpu.VMEM((384, 384), BF16),
            pltpu.VMEM((2, occ * 128, 2 * pairs), BF16),
            pltpu.VMEM((2, occ * 128, 2 * pairs), BF16),
            pltpu.VMEM((2, occ * 64, 2 * pairs), BF16),
        ]
        + [pltpu.VMEM((16, height, 128), F32) for unused in range(5) for height in (16, 24)]
        + [
            pltpu.VMEM((16, 3, 128), F32),
            pltpu.VMEM((16, 3, 128), F32),
            pltpu.SemaphoreType.DMA((slots,)),
            pltpu.SemaphoreType.DMA((4,)),
            pltpu.SemaphoreType.DMA((2,)),
            pltpu.SemaphoreType.DMA((2,)),
            pltpu.SemaphoreType.DMA((16,)),
            pltpu.SemaphoreType.DMA((16,)),
            pltpu.SemaphoreType.DMA((16,)),
            pltpu.SemaphoreType.DMA((16,)),
            pltpu.SemaphoreType.DMA((16,)),
            pltpu.SemaphoreType.DMA((16,)),
        ],
        compiler_params=pltpu.CompilerParams(
            collective_id=0, has_side_effects=True, vmem_limit_bytes=56 * 2**20
        ),
    )(eri, slot_tile, tile_mask, coef_mu.T, coef_lam.T)


def solution(mesh):
    in_specs = (P("row", None, None, "col"), P("row"), P(), P(), P("col", None))
    out_specs = P("col", "row")
    return jax.shard_map(
        per_device, mesh=mesh, in_specs=in_specs, out_specs=out_specs, check_vma=False
    )
```

time: 33.8 us -> 33.3 us (0.985)
  Pallas kernels: 33.1 us -> 32.6 us
    pallas_call x1, Pallas kernels: 33.1 us -> 32.6 us  [per_device(): pl.pallas_call(kernel, out_shape=pltpu.VMEM((1, 300), F32), in_specs=[pl....]
where the time goes in v3:
time: 33.3 us; the launch traced here: 33.2 us
  Pallas kernels  32.6 us (98%)
  local copies, waits for them, and re-layouts  0.56 us (2%)
    pallas_call x1, Pallas kernels, per_device(): pl.pallas_call(kernel, out_shape=pltpu.VMEM((1, 300), F32), in_specs=[pl....  32.6 us

profile of v3, /device:TPU:1, one launch (start us, length us, event | category | flops | bytes accessed | tf_op | source)
XLA Modules:
  0.0 33.2 jit_solution(17173095116736795246)
XLA Ops:
  0.0 32.6 %shard_map.55 = f32[1,300]{1,0:T(1,128)S(1)} custom-call(bf16[8,40,40,128]{3,2,1,0:T(8,128)(2,1)} %eri_hbm.1, s32[8]{0:T(128)} %tile_hbm.1, s32[225]{0:T(256)} %mask_hbm.1, bf16[8,600]{1,0:T(8,128)(2,1)} %bitcast.2, bf16[8,32]{1,0:T(8,128)(2,1)} %bitcast.3), custom_call_target="tpu_custom_call" | custom-call | tf_op jit(solution)/shard_map/pallas_call | solution.py:267
  32.6 0.6 %copy.7 = f32[1,300]{1,0:T(1,128)} copy(f32[1,300]{1,0:T(1,128)S(1)} %shard_map.55) | data formatting | bytes 2400

commit v4 on v3

--- a/solution.py
+++ b/solution.py
@@ -83,7 +83,7 @@
     eri_hbm, tile_hbm, mask_hbm, coef_hbm, lam_hbm, out_ref,
     tile_ref, mask_ref, coef_ref, lam_ref, ebuf, eturn, blocks, left, order, acc_a, acc_b, acc_c,
     theirs_p, theirs_q, mine_p, mine_q, core_p, core_q, send_p, send_q, got_p, got_q, send_z, got_z,
-    load_sem, small_sem, core_send, core_recv, p_send, p_recv, q_send, q_recv, z_send, z_recv,
+    load_sem, small_sem, core_send, core_recv, plane_send, plane_recv, z_send, z_recv,
 ):
     slots, edge, unused, pairs = ebuf.shape
     occ, basis = coef_ref.shape
@@ -146,15 +146,15 @@
                     start = ((half ^ c) * count + step) * 8
                     for i in range(occ):
                         g = (c * occ + i) * 8
-                        both = jnp.concatenate([sums[g : g + 8, :pairs], sums[g : g + 8, pairs:]], axis=0)
-                        high = both.astype(BF16)
-                        low = (both - high.astype(F32)).astype(BF16)
                         at = i * 2 * count * 8 + start
-                        acc[c, at : at + 16, :pairs] = high
-                        acc[c, at : at + 16, pairs:] = low
+                        acc[c, at : at + 8, :] = sums[g : g + 8, :pairs]
+                        acc[c, at + 8 : at + 16, :] = sums[g : g + 8, pairs:]
 
     def contract(acc, c, n):
-        right = acc[c, n * 256 : n * 256 + 256, :]
+        value = acc[c, n * 256 : n * 256 + 256, :]
+        high = value.astype(BF16)
+        low = (value - high.astype(F32)).astype(BF16)
+        right = jnp.concatenate([high, low], axis=1)
         return lax.dot_general(lam_twice, right, (((1,), (1,)), ((), ())), preferred_element_type=F32)
 
     def contract_wide(acc, c, dest):
@@ -184,27 +184,27 @@
         copy.start()
         return copy
 
-    def share(mine, theirs, send, got, send_sem, recv_sem):
-        copies = []
+    def to_plane(send, got, n, slot, other):
+        return pltpu.make_async_remote_copy(
+            src_ref=send.at[slot],
+            dst_ref=got.at[slot],
+            send_sem=plane_send.at[n],
+            recv_sem=plane_recv.at[n],
+            device_id=((other // 2) * 2 + core, (other % 2) * 16 + z),
+            device_id_type=MESH,
+        )
+
+    def share(mine, theirs, send, got, n):
         for d in PLANE_ORDER:
             other = place ^ d
             send[d] = mine[other] + theirs[other]
-            copy = pltpu.make_async_remote_copy(
-                src_ref=send.at[d],
-                dst_ref=got.at[d],
-                send_sem=send_sem.at[d],
-                recv_sem=recv_sem.at[d],
-                device_id=((other // 2) * 2 + core, (other % 2) * 16 + z),
-                device_id_type=MESH,
-            )
-            copy.start()
-            copies.append(copy)
-        return copies
+            to_plane(send, got, n, d, other).start()
+        return to_plane(send, got, n, pl.ds(1, 15), place ^ 1)
 
     def gather(mine, theirs, got, copies):
         total = mine[place] + theirs[place]
-        for copy, d in zip(copies, PLANE_ORDER):
-            copy.wait_recv()
+        copies.wait_recv()
+        for d in range(1, 16):
             total = total + got[d]
         return total
 
@@ -219,11 +219,11 @@
     contract_narrow(acc_c, 1 - core, theirs_q)
     second_swap = swap_cores(theirs_q, core_q, 1)
     first_swap.wait_recv()
-    p_copies = share(mine_p, core_p, send_p, got_p, p_send, p_recv)
+    p_copies = share(mine_p, core_p, send_p, got_p, 0)
     contract_wide(acc_b, core, mine_q)
     contract_narrow(acc_c, core, mine_q)
     second_swap.wait_recv()
-    q_copies = share(mine_q, core_q, send_q, got_q, q_send, q_recv)
+    q_copies = share(mine_q, core_q, send_q, got_q, 1)
 
     total = gather(mine_p, core_p, got_p, p_copies)
     send_z[:, 0, :] = total
@@ -231,22 +231,24 @@
     send_z[:, 1, :] = total[:16]
     send_z[0:8, 2, :] = total[16:]
     send_z[8:16, 2, :] = total[16:]
-    z_copies = []
+
+    def along_z(source, slot, other):
+        return pltpu.make_async_remote_copy(
+            src_ref=send_z.at[source],
+            dst_ref=got_z.at[slot],
+            send_sem=z_send,
+            recv_sem=z_recv,
+            device_id=(row, jhi * 16 + other),
+            device_id_type=MESH,
+        )
+
     for d in Z_ORDER:
         other = (z + d) % 16
-        copy = pltpu.make_async_remote_copy(
-            src_ref=send_z.at[other],
-            dst_ref=got_z.at[d],
-            send_sem=z_send.at[d],
-            recv_sem=z_recv.at[d],
-            device_id=(row, jhi * 16 + other),
-            device_id_type=MESH,
-        )
-        copy.start()
-        z_copies.append(copy)
+        along_z(other, d, other).start()
+    z_copies = along_z(pl.ds(1, 15), pl.ds(1, 15), (z + 1) % 16)
     final = send_z[z]
-    for copy, d in zip(z_copies, Z_ORDER):
-        copy.wait_recv()
+    z_copies.wait_recv()
+    for d in range(1, 16):
         final = final + got_z[d]
     flat = jnp.concatenate([final[k : k + 1, :] for k in range(3)], axis=1)
     high = flat.astype(BF16)
@@ -256,7 +258,7 @@
     terms = jnp.concatenate([high, middle, low], axis=0)
     picked = jnp.dot(terms, order[...], preferred_element_type=F32)
     out_ref[...] = (picked[0:1] + picked[1:2] + picked[2:3])[:, : out_ref.shape[1]]
-    for copy in [first_swap, second_swap] + p_copies + q_copies + z_copies:
+    for copy in (first_swap, second_swap, p_copies, q_copies, z_copies):
         copy.wait_send()
 
 
@@ -279,9 +281,9 @@
             pltpu.VMEM((nb, occ, 128), F32),
             pltpu.VMEM((2, 16 * occ, 2 * slots * edge), BF16),
             pltpu.VMEM((384, 384), BF16),
-            pltpu.VMEM((2, occ * 128, 2 * pairs), BF16),
-            pltpu.VMEM((2, occ * 128, 2 * pairs), BF16),
-            pltpu.VMEM((2, occ * 64, 2 * pairs), BF16),
+            pltpu.VMEM((2, occ * 128, pairs), F32),
+            pltpu.VMEM((2, occ * 128, pairs), F32),
+            pltpu.VMEM((2, occ * 64, pairs), F32),
         ]
         + [pltpu.VMEM((16, height, 128), F32) for unused in range(5) for height in (16, 24)]
         + [
@@ -291,12 +293,10 @@
             pltpu.SemaphoreType.DMA((4,)),
             pltpu.SemaphoreType.DMA((2,)),
             pltpu.SemaphoreType.DMA((2,)),
-            pltpu.SemaphoreType.DMA((16,)),
-            pltpu.SemaphoreType.DMA((16,)),
-            pltpu.SemaphoreType.DMA((16,)),
-            pltpu.SemaphoreType.DMA((16,)),
-            pltpu.SemaphoreType.DMA((16,)),
-            pltpu.SemaphoreType.DMA((16,)),
+            pltpu.SemaphoreType.DMA((2,)),
+            pltpu.SemaphoreType.DMA((2,)),
+            pltpu.SemaphoreType.DMA,
+            pltpu.SemaphoreType.DMA,
         ],
         compiler_params=pltpu.CompilerParams(
             collective_id=0, has_side_effects=True, vmem_limit_bytes=56 * 2**20

time: 33.3 us -> 32.3 us (0.970)
  Pallas kernels: 32.6 us -> 31.6 us
    pallas_call x1, Pallas kernels: 32.6 us -> 31.6 us  [per_device(): pl.pallas_call(kernel, out_shape=pltpu.VMEM((1, 300), F32), in_specs=[pl....]
where the time goes in v4:
time: 32.3 us; the launch traced here: 32.1 us
  Pallas kernels  31.6 us (98%)
  local copies, waits for them, and re-layouts  0.56 us (2%)
    pallas_call x1, Pallas kernels, per_device(): pl.pallas_call(kernel, out_shape=pltpu.VMEM((1, 300), F32), in_specs=[pl....  31.6 us

profile of v4, /device:TPU:1, one launch (start us, length us, event | category | flops | bytes accessed | tf_op | source)
XLA Modules:
  0.0 32.1 jit_solution(446368381495609247)
XLA Ops:
  0.0 31.6 %shard_map.55 = f32[1,300]{1,0:T(1,128)S(1)} custom-call(bf16[8,40,40,128]{3,2,1,0:T(8,128)(2,1)} %eri_hbm.1, s32[8]{0:T(128)} %tile_hbm.1, s32[225]{0:T(256)} %mask_hbm.1, bf16[8,600]{1,0:T(8,128)(2,1)} %bitcast.2, bf16[8,32]{1,0:T(8,128)(2,1)} %bitcast.3), custom_call_target="tpu_custom_call" | custom-call | tf_op jit(solution)/shard_map/pallas_call | solution.py:269
  31.6 0.6 %copy.7 = f32[1,300]{1,0:T(1,128)} copy(f32[1,300]{1,0:T(1,128)S(1)} %shard_map.55) | data formatting | bytes 2400

commit v5 on v4

--- a/solution.py
+++ b/solution.py
@@ -83,7 +83,7 @@
     eri_hbm, tile_hbm, mask_hbm, coef_hbm, lam_hbm, out_ref,
     tile_ref, mask_ref, coef_ref, lam_ref, ebuf, eturn, blocks, left, order, acc_a, acc_b, acc_c,
     theirs_p, theirs_q, mine_p, mine_q, core_p, core_q, send_p, send_q, got_p, got_q, send_z, got_z,
-    load_sem, small_sem, core_send, core_recv, plane_send, plane_recv, z_send, z_recv,
+    load_sem, small_sem, core_send, core_recv, plane_send, plane_recv, z_send, z_recv, told,
 ):
     slots, edge, unused, pairs = ebuf.shape
     occ, basis = coef_ref.shape
@@ -108,17 +108,32 @@
         copy.start()
 
     barrier = pltpu.get_barrier_semaphore()
-    pl.semaphore_signal(barrier, inc=1, device_id=sibling, device_id_type=MESH)
 
     def greet(d, unused):
         other = place ^ d
         pl.semaphore_signal(
-            barrier, inc=1, device_id=((other // 2) * 2 + core, (other % 2) * 16 + z), device_id_type=MESH
-        )
-        pl.semaphore_signal(barrier, inc=1, device_id=(row, jhi * 16 + (z ^ d)), device_id_type=MESH)
+            barrier, inc=1, device_id=((other // 2) * 2, (other % 2) * 16 + z), device_id_type=MESH
+        )
+        pl.semaphore_signal(
+            barrier, inc=1, device_id=(orbital * 2 + 1, jhi * 16 + (z ^ d)), device_id_type=MESH
+        )
         return unused
 
     lax.fori_loop(1, 16, greet, 0)
+
+    @pl.when(core == 1)
+    def _():
+        pl.semaphore_signal(barrier, inc=1, device_id=sibling, device_id_type=MESH)
+
+    def hear(teller, count):
+        @pl.when(core == teller)
+        def _():
+            pl.semaphore_wait(barrier, count)
+            pl.semaphore_signal(told, inc=1, device_id=sibling, device_id_type=MESH)
+
+        @pl.when(core != teller)
+        def _():
+            pl.semaphore_wait(told, 1)
 
     output_order(order, z, edge)
     for copy in smalls:
@@ -210,7 +225,7 @@
 
     transform(acc_a, 0, 8)
     contract_wide(acc_a, 1 - core, theirs_p)
-    pl.semaphore_wait(barrier, 31)
+    hear(0, 31)
     first_swap = swap_cores(theirs_p, core_p, 0)
     contract_wide(acc_a, core, mine_p)
     transform(acc_b, 8, 8)
@@ -242,6 +257,7 @@
             device_id_type=MESH,
         )
 
+    hear(1, 30)
     for d in Z_ORDER:
         other = (z + d) % 16
         along_z(other, d, other).start()
@@ -297,6 +313,7 @@
             pltpu.SemaphoreType.DMA((2,)),
             pltpu.SemaphoreType.DMA,
             pltpu.SemaphoreType.DMA,
+            pltpu.SemaphoreType.REGULAR,
         ],
         compiler_params=pltpu.CompilerParams(
             collective_id=0, has_side_effects=True, vmem_limit_bytes=56 * 2**20

time: 32.3 us -> 31.5 us (0.975)
  Pallas kernels: 31.6 us -> 30.8 us
    pallas_call x1, Pallas kernels: 31.6 us -> 30.8 us  [per_device(): pl.pallas_call(kernel, out_shape=pltpu.VMEM((1, 300), F32), in_specs=[pl....]
where the time goes in v5:
time: 31.5 us; the launch traced here: 31.4 us
  Pallas kernels  30.8 us (98%)
  local copies, waits for them, and re-layouts  0.56 us (2%)
    pallas_call x1, Pallas kernels, per_device(): pl.pallas_call(kernel, out_shape=pltpu.VMEM((1, 300), F32), in_specs=[pl....  30.8 us

profile of v5, /device:TPU:1, one launch (start us, length us, event | category | flops | bytes accessed | tf_op | source)
XLA Modules:
  0.0 31.4 jit_solution(18327308711802994611)
XLA Ops:
  0.0 30.8 %shard_map.55 = f32[1,300]{1,0:T(1,128)S(1)} custom-call(bf16[8,40,40,128]{3,2,1,0:T(8,128)(2,1)} %eri_hbm.1, s32[8]{0:T(128)} %tile_hbm.1, s32[225]{0:T(256)} %mask_hbm.1, bf16[8,600]{1,0:T(8,128)(2,1)} %bitcast.2, bf16[8,32]{1,0:T(8,128)(2,1)} %bitcast.3), custom_call_target="tpu_custom_call" | custom-call | tf_op jit(solution)/shard_map/pallas_call | solution.py:285
  30.8 0.6 %copy.7 = f32[1,300]{1,0:T(1,128)} copy(f32[1,300]{1,0:T(1,128)S(1)} %shard_map.55) | data formatting | bytes 2400

commit v6 on v5

--- a/solution.py
+++ b/solution.py
@@ -104,26 +104,28 @@
     for copy in smalls:
         copy.start()
     loads = [pltpu.make_async_copy(eri_hbm.at[s], ebuf.at[s], load_sem.at[s]) for s in range(slots)]
-    for copy in loads:
-        copy.start()
+    for n, copy in enumerate(loads):
+        copy.start(priority=int(n >= 4))
 
     barrier = pltpu.get_barrier_semaphore()
 
-    def greet(d, unused):
+    for d in PLANE_ORDER:
         other = place ^ d
         pl.semaphore_signal(
             barrier, inc=1, device_id=((other // 2) * 2, (other % 2) * 16 + z), device_id_type=MESH
         )
-        pl.semaphore_signal(
-            barrier, inc=1, device_id=(orbital * 2 + 1, jhi * 16 + (z ^ d)), device_id_type=MESH
-        )
-        return unused
-
-    lax.fori_loop(1, 16, greet, 0)
 
     @pl.when(core == 1)
     def _():
         pl.semaphore_signal(barrier, inc=1, device_id=sibling, device_id_type=MESH)
+
+    def greet(d, unused):
+        pl.semaphore_signal(
+            barrier, inc=1, device_id=(orbital * 2 + 1, jhi * 16 + (z + d) % 16), device_id_type=MESH
+        )
+        return unused
+
+    lax.fori_loop(1, 16, greet, 0)
 
     def hear(teller, count):
         @pl.when(core == teller)
@@ -210,10 +212,20 @@
         )
 
     def share(mine, theirs, send, got, n):
+        def give(slot, other):
+            send[slot] = mine[other] + theirs[other]
+            to_plane(send, got, n, slot, other).start()
+
+        @pl.when(place != 0)
+        def _():
+            give(place, 0)
+
         for d in PLANE_ORDER:
-            other = place ^ d
-            send[d] = mine[other] + theirs[other]
-            to_plane(send, got, n, d, other).start()
+
+            @pl.when(place != d)
+            def _():
+                give(d, place ^ d)
+
         return to_plane(send, got, n, pl.ds(1, 15), place ^ 1)
 
     def gather(mine, theirs, got, copies):
@@ -240,6 +252,7 @@
     second_swap.wait_recv()
     q_copies = share(mine_q, core_q, send_q, got_q, 1)
 
+    hear(1, 30)
     total = gather(mine_p, core_p, got_p, p_copies)
     send_z[:, 0, :] = total
     total = gather(mine_q, core_q, got_q, q_copies)
@@ -257,7 +270,6 @@
             device_id_type=MESH,
         )
 
-    hear(1, 30)
     for d in Z_ORDER:
         other = (z + d) % 16
         along_z(other, d, other).start()

time: 31.5 us -> 30.6 us (0.971)
  Pallas kernels: 30.8 us -> 29.6 us
    pallas_call x1, Pallas kernels: 30.8 us -> 29.6 us  [per_device(): pl.pallas_call(kernel, out_shape=pltpu.VMEM((1, 300), F32), in_specs=[pl....]
where the time goes in v6:
time: 30.6 us; the launch traced here: 30.2 us
  Pallas kernels  29.6 us (97%)
  local copies, waits for them, and re-layouts  0.56 us (2%)
    pallas_call x1, Pallas kernels, per_device(): pl.pallas_call(kernel, out_shape=pltpu.VMEM((1, 300), F32), in_specs=[pl....  29.6 us

profile of v6, /device:TPU:1, one launch (start us, length us, event | category | flops | bytes accessed | tf_op | source)
XLA Modules:
  0.0 30.2 jit_solution(15012045265067442413)
XLA Ops:
  0.0 29.6 %shard_map.55 = f32[1,300]{1,0:T(1,128)S(1)} custom-call(bf16[8,40,40,128]{3,2,1,0:T(8,128)(2,1)} %eri_hbm.1, s32[8]{0:T(128)} %tile_hbm.1, s32[225]{0:T(256)} %mask_hbm.1, bf16[8,600]{1,0:T(8,128)(2,1)} %bitcast.2, bf16[8,32]{1,0:T(8,128)(2,1)} %bitcast.3), custom_call_target="tpu_custom_call" | custom-call | tf_op jit(solution)/shard_map/pallas_call | solution.py:297
  29.6 0.6 %copy.7 = f32[1,300]{1,0:T(1,128)} copy(f32[1,300]{1,0:T(1,128)S(1)} %shard_map.55) | data formatting | bytes 2400

commit v7 on v6

--- a/solution.py
+++ b/solution.py
@@ -103,9 +103,16 @@
     ]
     for copy in smalls:
         copy.start()
-    loads = [pltpu.make_async_copy(eri_hbm.at[s], ebuf.at[s], load_sem.at[s]) for s in range(slots)]
-    for n, copy in enumerate(loads):
-        copy.start(priority=int(n >= 4))
+    group = slots // 2
+
+    def load(n, first, count):
+        return pltpu.make_async_copy(
+            eri_hbm.at[pl.ds(first, count)], ebuf.at[pl.ds(first, count)], load_sem.at[n]
+        )
+
+    for n in range(2):
+        for s in range(group):
+            load(n, n * group + s, 1).start(priority=n)
 
     barrier = pltpu.get_barrier_semaphore()
 
@@ -144,7 +151,8 @@
     lam_twice = second_factor(lam_ref, pairs, occ)
 
     for s in range(slots):
-        loads[s].wait()
+        if s % group == 0:
+            load(s // group, s, group).wait()
         eturn[:, s * edge : (s + 1) * edge, :] = jnp.swapaxes(ebuf[s], 0, 1)
 
     def transform(acc, first, count):
@@ -237,9 +245,9 @@
 
     transform(acc_a, 0, 8)
     contract_wide(acc_a, 1 - core, theirs_p)
+    contract_wide(acc_a, core, mine_p)
     hear(0, 31)
     first_swap = swap_cores(theirs_p, core_p, 0)
-    contract_wide(acc_a, core, mine_p)
     transform(acc_b, 8, 8)
     transform(acc_c, 16, 4)
     contract_wide(acc_b, 1 - core, theirs_q)
@@ -317,7 +325,7 @@
         + [
             pltpu.VMEM((16, 3, 128), F32),
             pltpu.VMEM((16, 3, 128), F32),
-            pltpu.SemaphoreType.DMA((slots,)),
+            pltpu.SemaphoreType.DMA((2,)),
             pltpu.SemaphoreType.DMA((4,)),
             pltpu.SemaphoreType.DMA((2,)),
             pltpu.SemaphoreType.DMA((2,)),

time: 30.6 us -> 30.5 us (level)
  no operation moved by 1% of the time
where the time goes in v7:
time: 30.5 us; the launch traced here: 30 us
  Pallas kernels  29.5 us (97%)
  local copies, waits for them, and re-layouts  0.56 us (2%)
    pallas_call x1, Pallas kernels, per_device(): pl.pallas_call(kernel, out_shape=pltpu.VMEM((1, 300), F32), in_specs=[pl....  29.5 us

profile of v7, /device:TPU:1, one launch (start us, length us, event | category | flops | bytes accessed | tf_op | source)
XLA Modules:
  0.0 30.0 jit_solution(16624501564915553917)
XLA Ops:
  0.0 29.5 %shard_map.55 = f32[1,300]{1,0:T(1,128)S(1)} custom-call(bf16[8,40,40,128]{3,2,1,0:T(8,128)(2,1)} %eri_hbm.1, s32[8]{0:T(128)} %tile_hbm.1, s32[225]{0:T(256)} %mask_hbm.1, bf16[8,600]{1,0:T(8,128)(2,1)} %bitcast.2, bf16[8,32]{1,0:T(8,128)(2,1)} %bitcast.3), custom_call_target="tpu_custom_call" | custom-call | tf_op jit(solution)/shard_map/pallas_call | solution.py:305
  29.5 0.6 %copy.7 = f32[1,300]{1,0:T(1,128)} copy(f32[1,300]{1,0:T(1,128)S(1)} %shard_map.55) | data formatting | bytes 2400
